TPU v7x, 32 devices: a whole 2x2x4 slice. The times are simulated.
32 devices in a mesh: tp: 2 (over x), dp: 16 (over z, y, core).
Axes of the slice: x: 2, y: 2, z: 4, core: 2. Of those that a mesh axis runs over, the one named last changes fastest.
Arguments:
- item_query: bfloat16 [2048, 2048], P('dp', 'tp'), may hold values from -20 to 20, as said below
- item_keys: bfloat16 [2048, 4, 2048], P('dp', None, 'tp'), may hold values from -20 to 20
- item_values: bfloat16 [2048, 4, 2048], P('dp', None, 'tp'), may hold values from -6 to 6
- item_out_weight: bfloat16 [2048, 4096], P('tp'), may hold values from -0.125 to 0.125
- item_residual: bfloat16 [2048, 4096], P('dp'), may hold values from -3 to 3
- cite_home: int32 [16384, 1], P('dp'), may hold values from 0 to 15; in each aligned block of 1024 rows (0 to 1023, 1024 to 2047, ...) at most 96 rows name the same one
- cite_row: int32 [16384], P('dp'), may hold values from 0 to 127
- seq_length: int32 [16], P('dp'), may hold values from 1 to 1024, 10240 in all
- user_gain: float32 [4096], replicated, may hold values from 0.1 to 1.9
- user_weight: bfloat16 [4096, 16, 384], P('dp', 'tp'), may hold values from -0.09375 to 0.09375
Outputs:
- user_qkv: bfloat16 [16384, 16, 384], P('dp', 'tp')
Inputs may be any that keep to these rules, and one draw needn't show every extreme that they name: `item_query`: in hidden draws some items' queries equal a multiple of keys at their last two tokens. `cite_home`: among the 1024 positions of one sequence at most 96 cite items of one home device, and some home device is cited exactly 96 times. `seq_length`: some sequence has all 1024 positions live.
All inputs are finite; a program needn't handle non-finite values. No bound on the sum of `seq_length` on one device may be relied on, other than what follows from the above.
Results may differ from a plain program's by a relative error of at most 0.0065.
Values may be sent and summed in bfloat16 or wider, within the bound.
A program may use at most 128 MiB of HBM per device.

v0:
```python
import math

import jax
import jax.numpy as jnp
from jax import lax
from jax.sharding import PartitionSpec as P

HEAD_DIM = 128


def per_device(
    item_query,
    item_keys,
    item_values,
    item_out_weight,
    item_residual,
    cite_home,
    cite_row,
    seq_length,
    user_gain,
    user_weight,
):
    count_items, width_heads = item_query.shape
    tokens_item = item_keys.shape[1]
    local_heads = width_heads // HEAD_DIM
    queries = item_query.reshape(count_items, local_heads, HEAD_DIM)
    keys_all = item_keys.reshape(count_items, tokens_item, local_heads, HEAD_DIM)
    values_all = item_values.reshape(count_items, tokens_item, local_heads, HEAD_DIM)
    scores = jnp.einsum("ihd,ithd->iht", queries, keys_all, preferred_element_type=jnp.float32) * (
        1.0 / math.sqrt(HEAD_DIM)
    )
    probs = jax.nn.softmax(scores, axis=-1).astype(jnp.bfloat16)
    attended = jnp.einsum("iht,ithd->ihd", probs, values_all, preferred_element_type=jnp.float32)
    attended = attended.astype(jnp.bfloat16).reshape(count_items, width_heads)
    partial_value = jnp.dot(attended, item_out_weight, preferred_element_type=jnp.float32)
    summed = lax.psum(partial_value, "tp")
    item_vec = (summed + item_residual.astype(jnp.float32)).astype(jnp.bfloat16)
    home_dev = cite_home[:, 0]
    length_seq = home_dev.shape[0]
    devices = lax.axis_size("dp")
    capacity = 3 * length_seq // (2 * devices)
    onehot = (home_dev[:, None] == jnp.arange(devices, dtype=jnp.int32)[None, :]).astype(jnp.int32)
    before = jnp.cumsum(onehot, axis=0) - onehot
    slot_index = jnp.sum(before * onehot, axis=1)
    target = home_dev * capacity + slot_index
    wanted = (
        jnp.zeros((devices * capacity,), jnp.int32)
        .at[target]
        .set(cite_row)
        .reshape(devices, capacity)
    )
    asked = lax.all_to_all(wanted, "dp", split_axis=0, concat_axis=0, tiled=True)
    looked = jnp.take(item_vec, asked.reshape(-1), axis=0).reshape(
        devices, capacity, item_vec.shape[1]
    )
    answers = lax.all_to_all(looked, "dp", split_axis=0, concat_axis=0, tiled=True)
    cited = jnp.take(answers.reshape(devices * capacity, item_vec.shape[1]), target, axis=0)
    values32 = cited.astype(jnp.float32)
    scale = lax.rsqrt(jnp.mean(values32 * values32, axis=1, keepdims=True) + 1e-05)
    normed = (values32 * scale * user_gain[None, :]).astype(jnp.bfloat16)
    shard_rows, user_heads, triple = user_weight.shape
    weight_flat = user_weight.reshape(shard_rows, user_heads * triple)
    projected = jnp.dot(
        normed,
        lax.all_gather(weight_flat, "dp", axis=0, tiled=True),
        preferred_element_type=jnp.float32,
    )
    live = jnp.arange(length_seq, dtype=jnp.int32) < seq_length[0]
    masked = jnp.where(live[:, None], projected, jnp.zeros_like(projected))
    return masked.astype(jnp.bfloat16).reshape(length_seq, user_heads, triple)


def solution(mesh):
    in_specs = (
        P("dp", "tp"),
        P("dp", None, "tp"),
        P("dp", None, "tp"),
        P("tp", None),
        P("dp", None),
        P("dp", None),
        P("dp"),
        P("dp"),
        P(),
        P("dp", "tp", None),
    )
    out_specs = P("dp", "tp", None)
    return jax.shard_map(
        per_device, mesh=mesh, in_specs=in_specs, out_specs=out_specs, check_vma=False
    )
```

profile of v0, /device:TPU:13, one launch (start us, length us, event | category | flops | bytes accessed | tf_op | source)
XLA Modules:
  0.0 491.8 jit_solution(15092317251637650228)
XLA Ops:
  7.4 0.0 copy-start
  7.4 0.0 all-reduce.2.cloned.1.call-start
  7.4 1.2 reshape.149
  8.6 2.4 fusion.11
  11.0 0.2 copy.19
  11.3 0.4 copy.20
  11.7 0.0 copy-done
  11.8 1.2 fusion.9
  13.0 0.0 copy-start.2
  13.0 0.0 copy-start.3
  13.0 6.1 %fusion.13 = f32[128,4096]{1,0:T(8,128)} fusion(bf16[1024,4096]{1,0:T(8,128)(2,1)} %param.13, bf16[16,8,8,128]{3,2,1,0:T(8,128)(2,1)S(1)} %bitcast.64), kind=kOutput, calls=%fused_computation.19 | convolution fusion | flops 1073741824 | bytes 10747904 | tf_op jit(solution)/shard_map/dot_general | solution.py:35
  19.1 0.0 all-reduce.2.cloned.1.call-update
  19.1 0.0 all-gather.2.cloned.1.call-start
  19.2 0.0 copy-done.2
  19.2 1.4 copy.25
  20.6 0.0 all-gather.2.cloned.1.call-update
  20.7 0.0 copy-done.3
  20.7 4.5 reduce-window.6
  25.2 0.1 slice.12
  25.3 0.1 copy.15
  25.5 0.1 copy.16
  25.5 0.1 broadcast_add_fusion
  25.7 4.5 scatter_custom_fusion
  30.2 0.1 all_to_all.9
  30.3 10.3 %all_to_all.14 = s32[16,1,96]{2,1,0:T(1,128)S(1)} all-to-all(s32[16,1,96]{2,1,0:T(1,128)S(1)} %all_to_all.9), channel_id=1, replica_groups=mesh['tp'=2,'dp'=16] {'dp'}, dimensions={0} | all-to-all | bytes 12288 | tf_op jit(solution)/shard_map/all_to_all | solution.py:52
  40.6 0.5 broadcast.90
  41.0 0.6 reduce.7
  41.6 0.1 reshape.116
  41.8 41.7 %all-reduce.2.cloned.1.call-done = f32[128,4096]{1,0:T(8,128)} async-done(((f32[128,4096]{1,0:T(8,128)}), f32[128,4096]{1,0:T(8,128)}) %all-reduce.2.cloned.1.call-update) | async-done | bytes 2097168 | tf_op jit(solution)/shard_map/psum | solution.py:36
  83.5 2.1 add_convert_fusion
  85.5 9.7 %gather_fusion = bf16[1536,4096]{1,0:T(8,128)(2,1)} fusion(bf16[128,4096]{1,0:T(8,128)(2,1)S(1)} %add_convert_fusion, s32[2048]{0:T(1024)S(1)} %pad_clamp_fusion), kind=kCustom, calls=%fused_computation | custom fusion | bytes 25171968 | tf_op jit(solution)/shard_map/jit(_take)/gather | solution.py:53
  95.2 10.8 %broadcast_select_fusion = bf16[16,96,4096]{2,1,0:T(8,128)(2,1)} fusion(bf16[16,96,4096]{2,1,0:T(8,128)(2,1)} %bitcast.61, pred[16,96]{1,0:T(8,128)(4,1)S(1)} %compare_and_fusion), kind=kLoop, calls=%fused_computation.9 | loop fusion | flops 6291456 | bytes 25167360 | tf_op jit(solution)/shard_map/jit(_take)/select_n | solution.py:53
  106.0 6.3 %all-to-all-start.1 = ((bf16[16,96,4096]{2,1,0:T(8,128)(2,1)}), bf16[16,96,4096]{2,1,0:T(8,128)(2,1)}, u32[]{:S(2)}, u32[]{:S(2)}) async-start(bf16[16,96,4096]{2,1,0:T(8,128)(2,1)} %broadcast_select_fusion), calls=%async_computation.1 | async-start | bytes 25165824 | tf_op jit(solution)/shard_map/all_to_all | solution.py:56
  113.1 305.8 %all-to-all-done.1 = bf16[16,96,4096]{2,1,0:T(8,128)(2,1)} async-done(((bf16[16,96,4096]{2,1,0:T(8,128)(2,1)}), bf16[16,96,4096]{2,1,0:T(8,128)(2,1)}, u32[]{:S(2)}, u32[]{:S(2)}) %all-to-all-start.1) | async-done | bytes 12582944 | tf_op jit(solution)/shard_map/all_to_all | solution.py:56
  418.9 21.2 %gather_fusion.1 = bf16[1024,4096]{1,0:T(8,128)(2,1)} fusion(bf16[1536,4096]{1,0:T(8,128)(2,1)} %bitcast.15, s32[1024]{0:T(1024)S(1)} %broadcast_clamp_fusion), kind=kCustom, calls=%fused_computation.1 | custom fusion | bytes 16781312 | tf_op jit(solution)/shard_map/jit(_take)/gather | solution.py:57
  440.1 0.0 copy-start.4
  440.1 5.7 %fusion = f32[1024]{0:T(1024)S(1)} fusion(bf16[1024,4096]{1,0:T(8,128)(2,1)} %gather_fusion.1, pred[1024]{0:T(1024)(128)(4,1)S(1)} %get-tuple-element.5), kind=kLoop, calls=%fused_computation.5 | loop fusion | flops 16776192 | bytes 8393728 | tf_op jit(solution)/shard_map/reduce_sum | solution.py:59
  445.9 0.0 all-gather.2.cloned.1.call-done
  445.9 0.0 copy-done.4
  445.9 0.0 copy-start.1
  445.9 34.1 %select_convert_fusion = bf16[1024,3072]{1,0:T(8,128)(2,1)S(1)} fusion(pred[1024]{0:T(1024)(128)(4,1)S(1)} %iota_compare_fusion.2, bf16[4096,3072]{1,0:T(8,128)(2,1)} %all-gather.2.cloned.1.call-done, f32[4096]{0:T(1024)S(1)} %copy-done.4, f32[1024]{0:T(1024)S(1)} %add_rsqrt_fusion, bf16[1024,4096]{1,0:T(8,128)(2,1)} %gather_fusion.1, ...), kind=kOutput, calls=%fused_computation.8 | convolution fusion | flops 25797066752 | bytes 39868416 | tf_op jit(solution)/shard_map/dot_general | solution.py:63
  480.1 4.3 copy.26
  484.4 0.0 copy-done.1
  (15 shorter events, 0.2 us)
Async XLA Ops:
  7.4 4.4 copy-start
  7.4 76.1 %all-reduce.2.cloned.1.call-start = ((), (), s32[]{:S(2)}) async-start(), calls=%async_computation.2 | async-start | bytes 4194304 | tf_op jit(solution)/shard_map/psum | solution.py:36
  13.0 6.2 %copy-start.2 = (bf16[256,8,384]{2,1,0:T(8,128)(2,1)S(1)}, bf16[256,8,384]{2,1,0:T(8,128)(2,1)}, u32[]{:S(2)}) copy-start(bf16[256,8,384]{2,1,0:T(8,128)(2,1)} %param.19) | copy-start | bytes 4718596
  13.0 7.6 %copy-start.3 = (s32[1024,1]{0,1:T(1,128)S(1)}, s32[1024,1]{0,1:T(1,128)}, u32[]{:S(2)}) copy-start(s32[1024,1]{0,1:T(1,128)} %param.15) | copy-start | bytes 12292
  19.1 426.8 %all-gather.2.cloned.1.call-start = ((), (), s32[]{:S(2)}) async-start(), calls=%async_computation.3 | async-start | bytes 26738688 | tf_op jit(solution)/shard_map/all_gather | solution.py:65
  106.0 312.9 %all-to-all-start.1 = ((bf16[16,96,4096]{2,1,0:T(8,128)(2,1)}), bf16[16,96,4096]{2,1,0:T(8,128)(2,1)}, u32[]{:S(2)}, u32[]{:S(2)}) async-start(bf16[16,96,4096]{2,1,0:T(8,128)(2,1)} %broadcast_select_fusion), calls=%async_computation.1 | async-start | bytes 25165824 | tf_op jit(solution)/shard_map/all_to_all | solution.py:56
  440.1 5.8 %copy-start.4 = (f32[4096]{0:T(1024)S(1)}, f32[4096]{0:T(1024)}, u32[]{:S(2)}) copy-start(f32[4096]{0:T(1024)} %param.18) | copy-start | bytes 49156
  445.9 38.5 %copy-start.1 = (bf16[128,4,1024]{2,1,0:T(4,128)(2,1)S(1)}, bf16[128,4,1024]{2,1,0:T(4,128)(2,1)}, u32[]{:S(2)}) copy-start(bf16[128,4,1024]{2,1,0:T(4,128)(2,1)} %param.12) | copy-start | bytes 3145732
Sparse Core Ops, SparseCore 0:
  19.3 64.1 all-reduce.1
Sparse Core Ops, SparseCore 1:
  21.2 227.1 all-gather.1
where the time goes:
time: 492 us
  waiting for transfers between devices  348 us (71%)
  local copies, waits for them, and re-layouts  43.9 us (9%)
  matrix products  43.9 us (9%)
  other arithmetic  24.1 us (5%)
  between operations  15.7 us (3%)
  blocking collectives  10.3 us (2%)
  starting transfers between devices  6.39 us (1%)
    all_to_all x1, waiting for transfers between devices, per_device(): lax.all_to_all(looked, 'dp', split_axis=0, concat_axis=0, tiled=True)  306 us
    psum x1, waiting for transfers between devices, per_device(): summed = lax.psum(partial_value, 'tp')  41.7 us
    dot_general x1, matrix products, per_device(): jnp.dot(normed, lax.all_gather(weight_flat, 'dp', axis=0, tiled=True), pr...  34.1 us
    gather x1, local copies, waits for them, and re-layouts, per_device(): jnp.take(answers.reshape(devices * capacity, item_vec.shape[1]), target,...  21.2 us
    select_n x2, other arithmetic, per_device(): jnp.take(item_vec, asked.reshape(-1), axis=0)  10.9 us
    all_to_all x1, blocking collectives, per_device(): lax.all_to_all(wanted, 'dp', split_axis=0, concat_axis=0, tiled=True)  10.3 us
  transfers between devices with their start and end apart: 3, of which 2 were waited for; matrix products, arithmetic and copies ran while one was open for 13% of the time, Pallas kernels for 0%

commit v1 on v0

v1 whole, which is shorter than its diff:
```python
import math

import jax
import jax.numpy as jnp
from jax import lax
from jax.sharding import PartitionSpec as P

HEAD_DIM = 128


def attend(item_query, item_keys, item_values):
    count_items, width_heads = item_query.shape
    tokens_item = item_keys.shape[1]
    local_heads = width_heads // HEAD_DIM
    queries = item_query.reshape(count_items, local_heads, HEAD_DIM)
    keys_all = item_keys.reshape(count_items, tokens_item, local_heads, HEAD_DIM)
    values_all = item_values.reshape(count_items, tokens_item, local_heads, HEAD_DIM)
    scores = jnp.einsum("ihd,ithd->iht", queries, keys_all, preferred_element_type=jnp.float32) * (
        1.0 / math.sqrt(HEAD_DIM)
    )
    probs = jax.nn.softmax(scores, axis=-1).astype(jnp.bfloat16)
    attended = jnp.einsum("iht,ithd->ihd", probs, values_all, preferred_element_type=jnp.float32)
    return attended.astype(jnp.bfloat16).reshape(count_items, width_heads)


def per_device(
    item_query,
    item_keys,
    item_values,
    item_out_weight,
    item_residual,
    cite_home,
    cite_row,
    seq_length,
    user_gain,
    user_weight,
):
    devices, halves = lax.axis_size("dp"), lax.axis_size("tp")
    count_items = item_query.shape[0]
    shard_rows, user_heads, triple = user_weight.shape
    groups = devices // user_heads
    by_head = jnp.repeat(jnp.swapaxes(user_weight, 0, 1), groups, axis=0)
    weight = lax.all_to_all(by_head, "dp", split_axis=0, concat_axis=0, tiled=True)
    weight = weight.reshape(devices * shard_rows, triple)

    attended = attend(item_query, item_keys, item_values)
    partial_value = jnp.dot(attended, item_out_weight, preferred_element_type=jnp.float32)
    summed = lax.psum_scatter(partial_value, "tp", scatter_dimension=0, tiled=True)
    rows_half = count_items // halves
    mine = lax.dynamic_slice_in_dim(item_residual, lax.axis_index("tp") * rows_half, rows_half, 0)
    values32 = (summed + mine.astype(jnp.float32)).astype(jnp.bfloat16).astype(jnp.float32)
    scale = lax.rsqrt(jnp.mean(values32 * values32, axis=1, keepdims=True) + 1e-05)
    normed = (values32 * scale * user_gain[None, :]).astype(jnp.bfloat16)
    normed = lax.all_gather(normed, "tp", axis=0, tiled=True)
    members = [[part + groups * j for j in range(user_heads)] for part in range(groups)]
    normed = lax.all_gather(normed, "dp", axis_index_groups=members, axis=0, tiled=True)
    projected = jnp.dot(normed, weight, preferred_element_type=jnp.float32).astype(jnp.bfloat16)
    table = lax.all_gather(projected, "dp", axis=0, tiled=True)
    table = table.reshape(user_heads, devices * count_items, triple)

    home = cite_home[:, 0]
    place = (home % groups) * (user_heads * count_items) + (home // groups) * count_items + cite_row
    live = jnp.arange(home.shape[0], dtype=jnp.int32) < seq_length[0]
    place = jnp.where(live, place, -1)
    chosen = (place[:, None] == jnp.arange(devices * count_items, dtype=jnp.int32)[None, :]).astype(jnp.bfloat16)
    return jnp.einsum("rn,hnc->rhc", chosen, table, preferred_element_type=jnp.float32).astype(jnp.bfloat16)


def solution(mesh):
    in_specs = (
        P("dp", "tp"),
        P("dp", None, "tp"),
        P("dp", None, "tp"),
        P("tp", None),
        P("dp", None),
        P("dp", None),
        P("dp"),
        P("dp"),
        P(),
        P("dp", "tp", None),
    )
    out_specs = P("dp", "tp", None)
    return jax.shard_map(
        per_device, mesh=mesh, in_specs=in_specs, out_specs=out_specs, check_vma=False
    )
```

time: 492 us -> 394 us (0.80)
  the two profiles are of different devices: /device:TPU:13 before, /device:TPU:1 now
where the time goes in v1:
time: 394 us
  waiting for transfers between devices  206 us (52%)
  blocking collectives  127 us (32%)
  matrix products  35.2 us (9%)
  between operations  13.9 us (4%)
  local copies, waits for them, and re-layouts  8.93 us (2%)
    all_to_all x1, blocking collectives, per_device(): lax.all_to_all(by_head, 'dp', split_axis=0, concat_axis=0, tiled=True)  127 us
    all_gather x1, waiting for transfers between devices, per_device(): table = lax.all_gather(projected, 'dp', axis=0, tiled=True)  98.5 us
    all_gather x1, waiting for transfers between devices, per_device(): lax.all_gather(normed, 'dp', axis_index_groups=members, axis=0, tiled=True)  51.8 us
    reduce_scatter x1, waiting for transfers between devices, per_device(): lax.psum_scatter(partial_value, 'tp', scatter_dimension=0, tiled=True)  34 us
    all_gather x1, waiting for transfers between devices, per_device(): normed = lax.all_gather(normed, 'tp', axis=0, tiled=True)  21.4 us
    dot_general x1, matrix products, per_device(): jnp.einsum('rn,hnc->rhc', chosen, table, preferred_element_type=jnp.float32)  15.8 us
    dot_general x1, matrix products, per_device(): jnp.dot(normed, weight, preferred_element_type=jnp.float32)  9.66 us
  transfers between devices with their start and end apart: 4, of which 4 were waited for; matrix products, arithmetic and copies ran while one was open for 0% of the time, Pallas kernels for 0%

profile of v1, /device:TPU:1, one launch (start us, length us, event | category | flops | bytes accessed | tf_op | source)
XLA Modules:
  0.0 393.9 jit_solution(12971824937308545099)
XLA Ops:
  6.5 0.0 copy-start
  6.5 0.0 reduce-scatter.2.cloned.1.call-start
  6.5 1.2 reshape.46
  7.8 2.4 fusion.12
  10.2 0.2 copy.17
  10.5 0.4 copy.18
  10.9 0.0 copy-done
  10.9 1.2 fusion.10
  12.2 0.0 copy-start.2
  12.2 0.0 copy-start.1
  12.2 6.1 %fusion.14 = f32[128,4096]{1,0:T(8,128)} fusion(bf16[1024,4096]{1,0:T(8,128)(2,1)} %param.13, bf16[16,8,8,128]{3,2,1,0:T(8,128)(2,1)S(1)} %bitcast.46), kind=kOutput, calls=%fused_computation.16 | convolution fusion | flops 1073741824 | bytes 10747904 | tf_op jit(solution)/shard_map/dot_general | solution.py:47
  18.3 0.0 reduce-scatter.2.cloned.1.call-update
  18.3 0.0 all-gather.4.cloned.1.call-start
  18.4 34.0 %reduce-scatter.2.cloned.1.call-done = f32[64,4096]{1,0:T(8,128)} async-done(((f32[128,4096]{1,0:T(8,128)}), f32[64,4096]{1,0:T(8,128)}) %reduce-scatter.2.cloned.1.call-update) | async-done | bytes 1048592 | tf_op jit(solution)/shard_map/reduce_scatter | solution.py:48
  52.4 1.6 fusion.7
  54.0 0.0 copy-done.2
  54.0 1.0 fusion.9
  55.0 0.0 all-gather.4.cloned.1.call-update
  55.0 0.0 all-gather.6.cloned.1.call-start
  55.1 21.4 %all-gather.4.cloned.1.call-done = bf16[128,4096]{1,0:T(8,128)(2,1)} async-done(((bf16[64,4096]{1,0:T(8,128)(2,1)}), bf16[128,4096]{1,0:T(8,128)(2,1)}) %all-gather.4.cloned.1.call-update) | async-done | bytes 1048592 | tf_op jit(solution)/shard_map/all_gather | solution.py:54
  76.5 0.0 all-gather.6.cloned.1.call-update
  76.5 0.0 all-gather.8.cloned.1.call-start
  76.6 0.0 copy-done.1
  76.6 0.2 copy.13
  76.8 0.4 broadcast_in_dim.3
  77.2 127.1 %all_to_all.5 = bf16[16,256,384]{2,1,0:T(8,128)(2,1)} all-to-all(bf16[16,256,384]{2,1,0:T(8,128)(2,1)S(1)} %bitcast.44), channel_id=1, replica_groups=mesh['tp'=2,'dp'=16] {'dp'}, dimensions={0} | all-to-all | bytes 6291456 | tf_op jit(solution)/shard_map/all_to_all | solution.py:43
  204.3 51.8 %all-gather.6.cloned.1.call-done = bf16[1024,4096]{1,0:T(8,128)(2,1)} async-done(((bf16[128,4096]{1,0:T(8,128)(2,1)}), bf16[1024,4096]{1,0:T(8,128)(2,1)}) %all-gather.6.cloned.1.call-update) | async-done | bytes 8388624 | tf_op jit(solution)/shard_map/all_gather | solution.py:56
  256.1 0.0 copy-start.3
  256.1 0.0 copy-start.4
  256.1 9.7 %convolution_convert_fusion = bf16[1024,384]{1,0:T(8,128)(2,1)} fusion(bf16[1024,4096]{1,0:T(8,128)(2,1)} %all-gather.6.cloned.1.call-done, bf16[4096,384]{1,0:T(8,128)(2,1)} %bitcast.45), kind=kOutput, calls=%fused_computation.5 | convolution fusion | flops 3221618688 | bytes 12320768 | tf_op jit(solution)/shard_map/dot_general | solution.py:57
  265.8 0.0 all-gather.8.cloned.1.call-update
  266.5 0.0 copy-done.3
  266.5 0.0 copy-done.4
  266.5 98.5 %all-gather.8.cloned.1.call-done = bf16[16384,384]{1,0:T(8,128)(2,1)} async-done(((bf16[1024,384]{1,0:T(8,128)(2,1)}), bf16[16384,384]{1,0:T(8,128)(2,1)}) %all-gather.8.cloned.1.call-update) | async-done | bytes 12582928 | tf_op jit(solution)/shard_map/all_gather | solution.py:58
  365.0 15.8 %fusion.4 = bf16[1024,8,384]{2,0,1:T(8,128)(2,1)S(1)} fusion(bf16[8,2048,384]{2,1,0:T(8,128)(2,1)} %bitcast.50, s32[1024]{0:T(1024)S(1)} %fusion.23), kind=kOutput, calls=%fused_computation.4 | convolution fusion | flops 12890144768 | bytes 18878464 | tf_op jit(solution)/shard_map/rn,hnc->rhc/dot_general | solution.py:66
  380.9 6.5 %copy.14 = bf16[1024,8,384]{2,1,0:T(8,128)(2,1)} copy(bf16[1024,8,384]{2,0,1:T(8,128)(2,1)S(1)} %fusion.4) | data formatting | bytes 12582912 | tf_op jit(solution)/shard_map/convert_element_type | solution.py:66
  (6 shorter events, 0.1 us)
Async XLA Ops:
  6.5 4.4 %copy-start = (bf16[128,4,1024]{2,1,0:T(4,128)(2,1)S(1)}, bf16[128,4,1024]{2,1,0:T(4,128)(2,1)}, u32[]{:S(2)}) copy-start(bf16[128,4,1024]{2,1,0:T(4,128)(2,1)} %param.12) | copy-start | bytes 3145732
  6.5 45.9 %reduce-scatter.2.cloned.1.call-start = ((), (), s32[]{:S(2)}) async-start(), calls=%async_computation.2 | async-start | bytes 3145728 | tf_op jit(solution)/shard_map/reduce_scatter | solution.py:48
  12.2 41.8 %copy-start.2 = (f32[4096]{0:T(1024)S(1)}, f32[4096]{0:T(1024)}, u32[]{:S(2)}) copy-start(f32[4096]{0:T(1024)} %param.18) | copy-start | bytes 49156
  12.2 64.4 %copy-start.1 = (bf16[256,8,384]{2,1,0:T(8,128)(2,1)S(1)}, bf16[256,8,384]{2,1,0:T(8,128)(2,1)}, u32[]{:S(2)}) copy-start(bf16[256,8,384]{2,1,0:T(8,128)(2,1)} %param.19) | copy-start | bytes 4718596
  18.3 58.2 %all-gather.4.cloned.1.call-start = ((), (), s32[]{:S(2)}) async-start(), calls=%async_computation.3 | async-start | bytes 1572864 | tf_op jit(solution)/shard_map/all_gather | solution.py:54
  55.0 201.1 %all-gather.6.cloned.1.call-start = ((), (), s32[]{:S(2)}) async-start(), calls=%async_computation.4 | async-start | bytes 9437184 | tf_op jit(solution)/shard_map/all_gather | solution.py:56
  76.5 288.5 %all-gather.8.cloned.1.call-start = ((), (), s32[]{:S(2)}) async-start(), calls=%async_computation.5 | async-start | bytes 13369344 | tf_op jit(solution)/shard_map/all_gather | solution.py:58
  256.1 10.3 %copy-start.3 = (s32[1024]{0:T(1024)S(1)}, s32[1024]{0:T(1024)}, u32[]{:S(2)}) copy-start(s32[1024]{0:T(1024)} %param.16) | copy-start | bytes 12292
  256.1 10.3 %copy-start.4 = (s32[1024,1]{0,1:T(1,128)S(1)}, s32[1024,1]{0,1:T(1,128)}, u32[]{:S(2)}) copy-start(s32[1024,1]{0,1:T(1,128)} %param.15) | copy-start | bytes 12292
Sparse Core Ops, SparseCore 0:
  18.4 33.9 reduce-scatter.1
  55.2 21.2 all-gather.3
  78.8 177.2 all-gather.5
  265.9 99.0 all-gather.7

commit v2 on v1

v2 whole, which is shorter than its diff:
```python
import functools
import math

import jax
import jax.numpy as jnp
from jax import lax
from jax.experimental import pallas as pl
from jax.experimental.pallas import tpu as pltpu
from jax.sharding import PartitionSpec as P

HEAD_DIM = 128
CORES = 2
PARTS = 4
EPS = 1e-05
MESH = pl.DeviceIdType.MESH


def attend(item_query, item_keys, item_values):
    count_items, width_heads = item_query.shape
    tokens_item = item_keys.shape[1]
    local_heads = width_heads // HEAD_DIM
    queries = item_query.reshape(count_items, local_heads, HEAD_DIM)
    keys_all = item_keys.reshape(count_items, tokens_item, local_heads, HEAD_DIM)
    values_all = item_values.reshape(count_items, tokens_item, local_heads, HEAD_DIM)
    scores = jnp.einsum("ihd,ithd->iht", queries, keys_all, preferred_element_type=jnp.float32) * (
        1.0 / math.sqrt(HEAD_DIM)
    )
    probs = jax.nn.softmax(scores, axis=-1).astype(jnp.bfloat16)
    attended = jnp.einsum("iht,ithd->ihd", probs, values_all, preferred_element_type=jnp.float32)
    return attended.astype(jnp.bfloat16).reshape(count_items, width_heads)


class Grid:
    def __init__(self, devices, halves, heads):
        self.halves = halves
        self.near = halves
        self.far = devices // (CORES * self.near)
        self.splits = math.gcd(self.far, heads)
        self.share = self.far // self.splits
        self.blocks = devices

    def here(self):
        index = lax.axis_index("dp")
        return index // (self.near * CORES), (index // CORES) % self.near, index % CORES

    def at(self, far, near, core):
        return (far * self.near + near) * CORES + core


def greet(grid, with_halves):
    far, near, core = grid.here()
    barrier = pltpu.get_barrier_semaphore()
    count = 0
    peers = [{"dp": grid.at((far + k) % grid.far, near, core)} for k in range(1, grid.far)]
    peers += [{"dp": grid.at(far, (near + k) % grid.near, core)} for k in range(1, grid.near)]
    peers += [{"dp": grid.at(far, near, 1 - core)}]
    if with_halves:
        half = lax.axis_index("tp")
        peers += [{"tp": (half + k) % grid.halves} for k in range(1, grid.halves)]
    for peer in peers:
        pl.semaphore_signal(barrier, inc=1, device_id=peer, device_id_type=MESH)
        count += 1
    pl.semaphore_wait(barrier, count)


class Spread:
    def __init__(self, grid, source_for, out_ref, send_sem, recv_sem, own_sem):
        self.grid, self.source_for, self.out = grid, source_for, out_ref
        self.send_sem, self.recv_sem, self.own_sem = send_sem, recv_sem, own_sem
        self.rows = out_ref.shape[1] // PARTS
        self.sent, self.count = [], [0] * PARTS

    def send(self, part, source, block, peer):
        slot = self.count[part]
        self.count[part] += 1
        copy = pltpu.make_async_remote_copy(
            src_ref=source.at[pl.ds(part * self.rows, self.rows)],
            dst_ref=self.out.at[block, pl.ds(part * self.rows, self.rows)],
            send_sem=self.send_sem.at[part, slot],
            recv_sem=self.recv_sem.at[part, block],
            device_id={"dp": peer},
            device_id_type=MESH,
        )
        copy.start()
        self.sent.append(copy)

    def arrived(self, part, block):
        view = self.out.at[block, pl.ds(part * self.rows, self.rows)]
        pltpu.make_async_copy(view, view, self.recv_sem.at[part, block]).wait()

    def onward(self, part, source, block, near_too):
        grid = self.grid
        far, near, core = grid.here()
        if near_too:
            for k in range(1, grid.near):
                self.send(part, source, block, grid.at(far, (near + k) % grid.near, core))
        self.send(part, source, block, grid.at(far, near, 1 - core))

    def first(self, part):
        grid = self.grid
        far, near, core = grid.here()
        mine = grid.at(far, near, core)
        for k in range(1, grid.far):
            to = (far + k) % grid.far
            self.send(part, self.source_for(to), mine, grid.at(to, near, core))
        if part == 0:
            self.own = pltpu.make_async_copy(self.source_for(far), self.out.at[mine], self.own_sem)
            self.own.start()

    def second(self, part):
        grid = self.grid
        far, near, core = grid.here()
        self.onward(part, self.source_for(far), grid.at(far, near, core), True)
        for k in range(1, grid.far):
            block = grid.at((far + grid.far - k) % grid.far, near, core)
            self.arrived(part, block)
            self.onward(part, self.out.at[block], block, True)

    def third(self, part):
        grid = self.grid
        far, near, core = grid.here()
        for k in range(1, grid.near):
            for j in range(grid.far):
                block = grid.at((far + grid.far - j) % grid.far, (near + grid.near - k) % grid.near, core)
                self.arrived(part, block)
                self.onward(part, self.out.at[block], block, False)

    def last(self):
        grid = self.grid
        far, near, core = grid.here()
        for part in range(PARTS):
            for j in range(grid.far):
                for k in range(grid.near):
                    self.arrived(part, grid.at((far + j) % grid.far, (near + k) % grid.near, 1 - core))
        for copy in self.sent:
            copy.wait_send()
        self.own.wait()

    def run(self):
        for step in range(PARTS + 2):
            if step < PARTS:
                self.first(step)
            if 1 <= step <= PARTS:
                self.second(step - 1)
            if 2 <= step:
                self.third(step - 2)
        self.last()


def share_kernel(grid, block_ref, out_ref, send_sem, recv_sem, own_sem):
    greet(grid, False)
    Spread(grid, lambda to: block_ref, out_ref, send_sem, recv_sem, own_sem).run()


def items_kernel(
    grid, send_ref, base_ref, gain_ref, weight_ref, items_out, weight_out,
    partial_buf, mine_buf, half_send, half_recv, item_send, item_recv, item_own,
    send_sem, recv_sem, own_sem,
):
    far, near, core = grid.here()
    half = lax.axis_index("tp")
    greet(grid, True)
    halves = []
    for k in range(1, grid.halves):
        peer = (half + k) % grid.halves
        copy = pltpu.make_async_remote_copy(
            src_ref=send_ref.at[peer],
            dst_ref=partial_buf.at[k - 1],
            send_sem=half_send.at[k - 1],
            recv_sem=half_recv.at[k - 1],
            device_id={"tp": peer},
            device_id_type=MESH,
        )
        copy.start()
        halves.append(copy)
    spread = Spread(grid, lambda to: weight_ref.at[to // grid.share], weight_out, send_sem, recv_sem, own_sem)
    for part in range(PARTS):
        spread.first(part)
    for copy in halves:
        copy.wait()

    step_rows = 16

    def norm(i, carry):
        rows = pl.ds(pl.multiple_of(i * step_rows, step_rows), step_rows)
        total = base_ref[rows, :]
        for k in range(1, grid.halves):
            total = total + partial_buf[k - 1, rows, :].astype(jnp.float32)
        vec = total.astype(jnp.bfloat16).astype(jnp.float32)
        scale = lax.rsqrt(jnp.mean(vec * vec, axis=1, keepdims=True) + EPS)
        mine_buf[rows, :] = (vec * scale * gain_ref[...]).astype(jnp.bfloat16)
        return carry

    lax.fori_loop(0, mine_buf.shape[0] // step_rows, norm, 0)

    column, rest = far // grid.share, far % grid.share
    sent = []

    def send_items(source, place, slot, peer):
        copy = pltpu.make_async_remote_copy(
            src_ref=source,
            dst_ref=items_out.at[place, half],
            send_sem=item_send.at[slot],
            recv_sem=item_recv.at[place, half],
            device_id=peer,
            device_id_type=MESH,
        )
        copy.start()
        sent.append(copy)

    def arrived(place, part):
        view = items_out.at[place, part]
        pltpu.make_async_copy(view, view, item_recv.at[place, part]).wait()

    slot = 0
    for k in range(1, grid.splits):
        to = ((column + k) % grid.splits) * grid.share + rest
        send_items(mine_buf, column, slot, {"dp": grid.at(to, near, core)})
        slot += 1
    own = pltpu.make_async_copy(mine_buf, items_out.at[column, half], item_own)
    own.start()
    for k in range(1, grid.halves):
        send_items(mine_buf, column, slot, {"tp": (half + k) % grid.halves})
        slot += 1
    for part in range(PARTS):
        spread.second(part)
    for j in range(1, grid.splits):
        place = (column + grid.splits - j) % grid.splits
        arrived(place, half)
        for k in range(1, grid.halves):
            send_items(items_out.at[place, half], place, slot, {"tp": (half + k) % grid.halves})
            slot += 1
    for part in range(PARTS):
        spread.third(part)
    for k in range(1, grid.halves):
        for j in range(grid.splits):
            arrived((column + j) % grid.splits, (half + k) % grid.halves)
    for copy in sent:
        copy.wait_send()
    own.wait()
    spread.last()


def spread_sems(grid):
    sends = grid.far - 1 + grid.far * (grid.near - 1) + grid.far * grid.near
    return [
        pltpu.SemaphoreType.DMA((PARTS, sends)),
        pltpu.SemaphoreType.DMA((PARTS, grid.blocks)),
        pltpu.SemaphoreType.DMA,
    ]


def per_device(
    item_query,
    item_keys,
    item_values,
    item_out_weight,
    item_residual,
    cite_home,
    cite_row,
    seq_length,
    user_gain,
    user_weight,
):
    devices, halves = lax.axis_size("dp"), lax.axis_size("tp")
    count_items = item_query.shape[0]
    shard_rows, user_heads, triple = user_weight.shape
    grid = Grid(devices, halves, user_heads)
    splits, share, near, far = grid.splits, grid.share, grid.near, grid.far
    columns = user_heads * triple // splits
    width = item_residual.shape[1]
    rows_half = count_items // halves
    half = lax.axis_index("tp")
    any_space = pl.BlockSpec(memory_space=pl.ANY)
    in_vmem = pl.BlockSpec(memory_space=pltpu.VMEM)

    by_column = jnp.swapaxes(user_weight.reshape(shard_rows, splits, columns), 0, 1)
    attended = attend(item_query, item_keys, item_values)
    partial_value = jnp.dot(attended, item_out_weight, preferred_element_type=jnp.float32)
    to_send = partial_value.astype(jnp.bfloat16).reshape(halves, rows_half, width)
    base = lax.dynamic_slice_in_dim(partial_value, half * rows_half, rows_half, 0) + lax.dynamic_slice_in_dim(
        item_residual, half * rows_half, rows_half, 0
    ).astype(jnp.float32)
    sends = splits - 1 + splits * (halves - 1)
    normed, weight = pl.pallas_call(
        functools.partial(items_kernel, grid),
        out_shape=(
            jax.ShapeDtypeStruct((splits, halves, rows_half, width), jnp.bfloat16),
            jax.ShapeDtypeStruct((devices, shard_rows, columns), jnp.bfloat16),
        ),
        in_specs=[any_space, in_vmem, in_vmem, any_space],
        out_specs=(any_space, any_space),
        scratch_shapes=[
            pltpu.VMEM((halves - 1, rows_half, width), jnp.bfloat16),
            pltpu.VMEM((rows_half, width), jnp.bfloat16),
            pltpu.SemaphoreType.DMA((halves - 1,)),
            pltpu.SemaphoreType.DMA((halves - 1,)),
            pltpu.SemaphoreType.DMA((sends,)),
            pltpu.SemaphoreType.DMA((splits, halves)),
            pltpu.SemaphoreType.DMA,
        ]
        + spread_sems(grid),
        compiler_params=pltpu.CompilerParams(
            collective_id=0, has_side_effects=True, vmem_limit_bytes=24 << 20
        ),
        name="gather_items",
    )(to_send, base, user_gain[None, :], by_column)

    normed = normed.reshape(splits * count_items, width)
    weight = weight.reshape(devices * shard_rows, columns)
    projected = jnp.dot(normed, weight, preferred_element_type=jnp.float32).astype(jnp.bfloat16)
    table = pl.pallas_call(
        functools.partial(share_kernel, grid),
        out_shape=jax.ShapeDtypeStruct((devices,) + projected.shape, jnp.bfloat16),
        in_specs=[any_space],
        out_specs=any_space,
        scratch_shapes=spread_sems(grid),
        compiler_params=pltpu.CompilerParams(collective_id=1, has_side_effects=True),
        name="gather_table",
    )(projected)
    table = table.reshape(splits, devices * count_items, columns)

    home = cite_home[:, 0]
    home_far, home_near, home_core = home // (near * CORES), (home // CORES) % near, home % CORES
    block = ((home_far % share) * near + home_near) * CORES + home_core
    place = (block * splits + home_far // share) * count_items + cite_row
    live = jnp.arange(home.shape[0], dtype=jnp.int32) < seq_length[0]
    place = jnp.where(live, place, -1)
    chosen = (place[:, None] == jnp.arange(devices * count_items, dtype=jnp.int32)[None, :]).astype(jnp.bfloat16)
    out = jnp.einsum("rn,snc->rsc", chosen, table, preferred_element_type=jnp.float32).astype(jnp.bfloat16)
    return out.reshape(home.shape[0], user_heads, triple)


def solution(mesh):
    in_specs = (
        P("dp", "tp"),
        P("dp", None, "tp"),
        P("dp", None, "tp"),
        P("tp", None),
        P("dp", None),
        P("dp", None),
        P("dp"),
        P("dp"),
        P(),
        P("dp", "tp", None),
    )
    out_specs = P("dp", "tp", None)
    return jax.shard_map(
        per_device, mesh=mesh, in_specs=in_specs, out_specs=out_specs, check_vma=False
    )
```

time: 394 us -> 248 us (0.63)
  waiting for transfers between devices: 206 us -> 0 us
  Pallas kernels: 0 us -> 198 us
  blocking collectives: 127 us -> 0 us
  between operations: 13.9 us -> 0.94 us
  local copies, waits for them, and re-layouts: 8.93 us -> 15.4 us
    pallas_call x0 -> x2, Pallas kernels: none -> 198 us  [the longest x1 102 us: per_device(): pl.pallas_call(functools.partial(share_kernel, grid), out_shape=jax.Shape...]
    all_gather x3 -> x0, waiting for transfers between devices: 172 us -> none  [the longest x1 98.5 us: per_device(): table = lax.all_gather(projected, 'dp', axis=0, tiled=True)]
    all_to_all x1 -> x0, blocking collectives: 127 us -> none  [per_device(): lax.all_to_all(by_head, 'dp', split_axis=0, concat_axis=0, tiled=True)]
    reduce_scatter x1 -> x0, waiting for transfers between devices: 34 us -> none  [per_device(): lax.psum_scatter(partial_value, 'tp', scatter_dimension=0, tiled=True)]
    reshape x0 -> x2, local copies, waits for them, and re-layouts: none -> 10.8 us  [the longest x1 9.06 us: per_device(): return out.reshape(home.shape[0], user_heads, triple)]
    convert_element_type x1 -> x0, local copies, waits for them, and re-layouts: 6.47 us -> none  [per_device(): jnp.einsum('rn,hnc->rhc', chosen, table, preferred_element_type=jnp.float32)]
    dot_general x1, matrix products: 9.66 us -> 4.3 us  [per_device(): jnp.dot(normed, weight, preferred_element_type=jnp.float32)]
  transfers between devices with their start and end apart: 4 -> 0, of which waited for: 4 -> 0; matrix products, arithmetic and copies ran while one was open for 0% -> 0% of each run, Pallas kernels for 0% -> 0%
where the time goes in v2:
time: 248 us; the launch traced here: 247 us
  Pallas kernels  198 us (80%)
  matrix products  32.3 us (13%)
  local copies, waits for them, and re-layouts  15.4 us (6%)
    pallas_call x1, Pallas kernels, per_device(): pl.pallas_call(functools.partial(share_kernel, grid), out_shape=jax.Shape...  102 us
    pallas_call x1, Pallas kernels, per_device(): pl.pallas_call(functools.partial(items_kernel, grid), out_shape=(jax.Shap...  95.7 us
    dot_general x1, matrix products, per_device(): jnp.einsum('rn,snc->rsc', chosen, table, preferred_element_type=jnp.float32)  18.8 us
    reshape x1, local copies, waits for them, and re-layouts, per_device(): return out.reshape(home.shape[0], user_heads, triple)  9.06 us

profile of v2, /device:TPU:1, one launch (start us, length us, event | category | flops | bytes accessed | tf_op | source)
XLA Modules:
  0.0 247.2 jit_solution(18006351039362882613)
XLA Ops:
  0.0 0.0 copy-start
  0.0 0.0 copy-start.2
  0.8 0.7 fusion.24
  1.5 1.1 reshape.49
  2.7 3.2 %fusion.9 = f32[128,8,1,4]{3,2,1,0:T(1,128)} fusion(bf16[128,8,128,1]{2,3,1,0:T(2,128)(2,1)S(1)} %reshape.49, bf16[128,4,1024]{2,1,0:T(4,128)(2,1)} %param.11), kind=kOutput, calls=%fused_computation.9 | convolution fusion | flops 1048576 | bytes 1327104 | tf_op jit(solution)/shard_map/ihd,ithd->iht/dot_general | solution.py:25
  5.9 1.2 copy.23
  7.2 0.4 copy.24
  7.6 0.0 copy-done
  7.6 1.2 fusion.7
  8.9 0.0 copy-done.2
  8.9 1.9 copy.17
  10.8 1.7 copy.18
  12.5 0.0 copy-start.3
  12.5 0.0 copy-start.1
  12.5 4.7 %fusion.30 = (bf16[128,4096]{1,0:T(8,128)(2,1)S(1)}, f32[128,4096]{1,0:T(8,128)S(1)}) fusion(bf16[1024,4096]{1,0:T(8,128)(2,1)} %param.13, bf16[16,8,8,128]{3,2,1,0:T(8,128)(2,1)S(1)} %bitcast.58), kind=kOutput, calls=%fused_computation.46 | convolution fusion | flops 1074266112 | bytes 11796480 | tf_op jit(solution)/shard_map/dot_general | solution.py:279
  17.3 0.0 copy-done.3
  17.3 0.1 convert_add_fusion.base_ref
  17.4 0.0 copy-done.1
  17.4 95.7 %gather_items.1 = (bf16[4,2,64,4096]{3,2,1,0:T(8,128)(2,1)S(1)}, bf16[16,256,768]{2,1,0:T(8,128)(2,1)S(1)}) custom-call(bf16[2,64,4096]{2,1,0:T(8,128)(2,1)S(1)} %bitcast.51, f32[64,4096]{1,0:T(8,128)S(1)} %convert_add_fusion.base_ref, f32[1,4096]{1,0:T(1,128)S(1)} %bitcast.52, bf16[4,256,768]{2,1,0:T(8,128)(2,1)S(1)} %bitcast.50), custom_call_target="tpu_custom_call" | custom-call | tf_op jit(solution)/shard_map/gather_items/pallas_call | solution.py:285
  113.2 4.3 %convolution_convert_fusion.block_ref = bf16[512,768]{1,0:T(8,128)(2,1)} fusion(bf16[512,4096]{1,0:T(8,128)(2,1)S(1)} %bitcast.54, bf16[4096,768]{1,0:T(8,128)(2,1)S(1)} %bitcast.53), kind=kOutput, calls=%fused_computation.5 | convolution fusion | flops 3221618688 | bytes 11272192 | tf_op jit(solution)/shard_map/dot_general | solution.py:311
  117.5 101.9 %gather_table.1 = bf16[16,512,768]{2,1,0:T(8,128)(2,1)} custom-call(bf16[512,768]{1,0:T(8,128)(2,1)} %convolution_convert_fusion.block_ref), custom_call_target="tpu_custom_call" | custom-call | tf_op jit(solution)/shard_map/gather_table/pallas_call | solution.py:312
  219.3 18.8 %fusion.4 = bf16[1024,4,768]{0,2,1:T(8,128)(2,1)} fusion(bf16[4,2048,768]{2,1,0:T(8,128)(2,1)} %bitcast.55, s32[1024]{0:T(1024)S(1)} %fusion.24), kind=kOutput, calls=%fused_computation.4 | convolution fusion | flops 12890144768 | bytes 18878464 | tf_op jit(solution)/shard_map/rn,snc->rsc/dot_general | solution.py:330
  238.2 9.1 %copy.20 = bf16[1024,8,384]{2,1,0:T(8,128)(2,1)} copy(bf16[1024,8,384]{0,2,1:T(8,128)(2,1)} %bitcast.56) | data formatting | bytes 12582912 | tf_op jit(solution)/shard_map/reshape | solution.py:331
  (4 shorter events, 0.1 us)
Async XLA Ops:
  0.0 7.6 %copy-start = (bf16[128,4,1024]{2,1,0:T(4,128)(2,1)S(1)}, bf16[128,4,1024]{2,1,0:T(4,128)(2,1)}, u32[]{:S(2)}) copy-start(bf16[128,4,1024]{2,1,0:T(4,128)(2,1)} %param.12) | copy-start | bytes 3145732
  0.0 8.9 %copy-start.2 = (bf16[256,8,384]{2,1,0:T(8,128)(2,1)S(1)}, bf16[256,8,384]{2,1,0:T(8,128)(2,1)}, u32[]{:S(2)}) copy-start(bf16[256,8,384]{2,1,0:T(8,128)(2,1)} %param.19) | copy-start | bytes 4718596
  12.5 4.8 %copy-start.3 = (bf16[128,4096]{1,0:T(8,128)(2,1)S(1)}, bf16[128,4096]{1,0:T(8,128)(2,1)}, u32[]{:S(2)}) copy-start(bf16[128,4096]{1,0:T(8,128)(2,1)} %param.14) | copy-start | bytes 3145732
  12.5 4.9 %copy-start.1 = (f32[4096]{0:T(1024)S(1)}, f32[4096]{0:T(1024)}, u32[]{:S(2)}) copy-start(f32[4096]{0:T(1024)} %param.18) | copy-start | bytes 49156

commit v3 on v2

--- a/solution.py
+++ b/solution.py
@@ -10,7 +10,9 @@
 
 HEAD_DIM = 128
 CORES = 2
-PARTS = 4
+TABLE_PARTS = 8
+WEIGHT_PARTS = 4
+ITEM_ROWS = 16
 EPS = 1e-05
 MESH = pl.DeviceIdType.MESH
 
@@ -45,6 +47,24 @@
 
     def at(self, far, near, core):
         return (far * self.near + near) * CORES + core
+
+
+def nearest(place, count):
+    order = [sorted(range(count), key=lambda other: (abs(other - at), other))[1:] for at in range(count)]
+    found = []
+    for k in range(count - 1):
+        other = order[0][k]
+        for at in range(1, count):
+            other = jnp.where(place == at, order[at][k], other)
+        found.append(other)
+    return found
+
+
+def beyond(place, origin, count):
+    up = origin < place
+    to = jnp.where(up, place + 1, place - 1)
+    ok = jnp.logical_and(to >= 0, to < count)
+    return jnp.clip(to, 0, count - 1), ok
 
 
 def greet(grid, with_halves):
@@ -64,13 +84,14 @@
 
 
 class Spread:
-    def __init__(self, grid, source_for, out_ref, send_sem, recv_sem, own_sem):
+    def __init__(self, grid, parts, chain, source_for, out_ref, send_sem, recv_sem, own_sem):
         self.grid, self.source_for, self.out = grid, source_for, out_ref
         self.send_sem, self.recv_sem, self.own_sem = send_sem, recv_sem, own_sem
-        self.rows = out_ref.shape[1] // PARTS
-        self.sent, self.count = [], [0] * PARTS
-
-    def send(self, part, source, block, peer):
+        self.chain = chain
+        self.parts, self.rows = parts, out_ref.shape[1] // parts
+        self.sent, self.count, self.maybe = [], [0] * parts, []
+
+    def send(self, part, source, block, peer, when=None):
         slot = self.count[part]
         self.count[part] += 1
         copy = pltpu.make_async_remote_copy(
@@ -81,8 +102,12 @@
             device_id={"dp": peer},
             device_id_type=MESH,
         )
-        copy.start()
-        self.sent.append(copy)
+        if when is None:
+            copy.start()
+            self.sent.append(copy)
+        else:
+            pl.when(when)(copy.start)
+            self.maybe.append((when, copy))
 
     def arrived(self, part, block):
         view = self.out.at[block, pl.ds(part * self.rows, self.rows)]
@@ -100,9 +125,15 @@
         grid = self.grid
         far, near, core = grid.here()
         mine = grid.at(far, near, core)
-        for k in range(1, grid.far):
-            to = (far + k) % grid.far
-            self.send(part, self.source_for(to), mine, grid.at(to, near, core))
+        if self.chain:
+            for step in (1, -1):
+                to = jnp.clip(far + step, 0, grid.far - 1)
+                there = far + step < grid.far if step > 0 else far + step >= 0
+                self.send(part, self.source_for(to), mine, grid.at(to, near, core), there)
+        else:
+            for k in range(1, grid.far):
+                to = (far + k) % grid.far
+                self.send(part, self.source_for(to), mine, grid.at(to, near, core))
         if part == 0:
             self.own = pltpu.make_async_copy(self.source_for(far), self.out.at[mine], self.own_sem)
             self.own.start()
@@ -111,9 +142,12 @@
         grid = self.grid
         far, near, core = grid.here()
         self.onward(part, self.source_for(far), grid.at(far, near, core), True)
-        for k in range(1, grid.far):
-            block = grid.at((far + grid.far - k) % grid.far, near, core)
+        for origin in nearest(far, grid.far):
+            block = grid.at(origin, near, core)
             self.arrived(part, block)
+            if self.chain:
+                to, there = beyond(far, origin, grid.far)
+                self.send(part, self.out.at[block], block, grid.at(to, near, core), there)
             self.onward(part, self.out.at[block], block, True)
 
     def third(self, part):
@@ -128,19 +162,21 @@
     def last(self):
         grid = self.grid
         far, near, core = grid.here()
-        for part in range(PARTS):
+        for part in range(self.parts):
             for j in range(grid.far):
                 for k in range(grid.near):
                     self.arrived(part, grid.at((far + j) % grid.far, (near + k) % grid.near, 1 - core))
         for copy in self.sent:
             copy.wait_send()
+        for when, copy in self.maybe:
+            pl.when(when)(copy.wait_send)
         self.own.wait()
 
     def run(self):
-        for step in range(PARTS + 2):
-            if step < PARTS:
+        for step in range(self.parts + 2):
+            if step < self.parts:
                 self.first(step)
-            if 1 <= step <= PARTS:
+            if 1 <= step <= self.parts:
                 self.second(step - 1)
             if 2 <= step:
                 self.third(step - 2)
@@ -149,7 +185,7 @@
 
 def share_kernel(grid, block_ref, out_ref, send_sem, recv_sem, own_sem):
     greet(grid, False)
-    Spread(grid, lambda to: block_ref, out_ref, send_sem, recv_sem, own_sem).run()
+    Spread(grid, TABLE_PARTS, True, lambda to: block_ref, out_ref, send_sem, recv_sem, own_sem).run()
 
 
 def items_kernel(
@@ -173,79 +209,86 @@
         )
         copy.start()
         halves.append(copy)
-    spread = Spread(grid, lambda to: weight_ref.at[to // grid.share], weight_out, send_sem, recv_sem, own_sem)
-    for part in range(PARTS):
+    spread = Spread(grid, WEIGHT_PARTS, False, lambda to: weight_ref.at[to // grid.share], weight_out, send_sem, recv_sem, own_sem)
+    for part in range(WEIGHT_PARTS):
         spread.first(part)
     for copy in halves:
         copy.wait()
 
-    step_rows = 16
-
-    def norm(i, carry):
-        rows = pl.ds(pl.multiple_of(i * step_rows, step_rows), step_rows)
+    column, rest = far // grid.share, far % grid.share
+    parts = mine_buf.shape[0] // ITEM_ROWS
+    sent, maybe, count = [], [], [0] * parts
+
+    def send_items(part, source, place, peer, when=None):
+        rows = pl.ds(part * ITEM_ROWS, ITEM_ROWS)
+        copy = pltpu.make_async_remote_copy(
+            src_ref=source.at[rows],
+            dst_ref=items_out.at[place, half, rows],
+            send_sem=item_send.at[part, count[part]],
+            recv_sem=item_recv.at[part, place, half],
+            device_id=peer,
+            device_id_type=MESH,
+        )
+        count[part] += 1
+        if when is None:
+            copy.start()
+            sent.append(copy)
+        else:
+            pl.when(when)(copy.start)
+            maybe.append((when, copy))
+
+    def arrived(part, place, origin):
+        view = items_out.at[place, origin, pl.ds(part * ITEM_ROWS, ITEM_ROWS)]
+        pltpu.make_async_copy(view, view, item_recv.at[part, place, origin]).wait()
+
+    for part in range(parts):
+        rows = pl.ds(part * ITEM_ROWS, ITEM_ROWS)
         total = base_ref[rows, :]
         for k in range(1, grid.halves):
             total = total + partial_buf[k - 1, rows, :].astype(jnp.float32)
         vec = total.astype(jnp.bfloat16).astype(jnp.float32)
         scale = lax.rsqrt(jnp.mean(vec * vec, axis=1, keepdims=True) + EPS)
         mine_buf[rows, :] = (vec * scale * gain_ref[...]).astype(jnp.bfloat16)
-        return carry
-
-    lax.fori_loop(0, mine_buf.shape[0] // step_rows, norm, 0)
-
-    column, rest = far // grid.share, far % grid.share
-    sent = []
-
-    def send_items(source, place, slot, peer):
-        copy = pltpu.make_async_remote_copy(
-            src_ref=source,
-            dst_ref=items_out.at[place, half],
-            send_sem=item_send.at[slot],
-            recv_sem=item_recv.at[place, half],
-            device_id=peer,
-            device_id_type=MESH,
-        )
-        copy.start()
-        sent.append(copy)
-
-    def arrived(place, part):
-        view = items_out.at[place, part]
-        pltpu.make_async_copy(view, view, item_recv.at[place, part]).wait()
-
-    slot = 0
-    for k in range(1, grid.splits):
-        to = ((column + k) % grid.splits) * grid.share + rest
-        send_items(mine_buf, column, slot, {"dp": grid.at(to, near, core)})
-        slot += 1
+        for step in (1, -1):
+            to = jnp.clip(column + step, 0, grid.splits - 1) * grid.share + rest
+            there = column + step < grid.splits if step > 0 else column + step >= 0
+            send_items(part, mine_buf, column, {"dp": grid.at(to, near, core)}, there)
+        for k in range(1, grid.halves):
+            send_items(part, mine_buf, column, {"tp": (half + k) % grid.halves})
     own = pltpu.make_async_copy(mine_buf, items_out.at[column, half], item_own)
     own.start()
-    for k in range(1, grid.halves):
-        send_items(mine_buf, column, slot, {"tp": (half + k) % grid.halves})
-        slot += 1
-    for part in range(PARTS):
-        spread.second(part)
-    for j in range(1, grid.splits):
-        place = (column + grid.splits - j) % grid.splits
-        arrived(place, half)
+    for step in range(max(parts, WEIGHT_PARTS)):
+        if step < WEIGHT_PARTS:
+            spread.second(step)
+        if step < parts:
+            for place in nearest(column, grid.splits):
+                arrived(step, place, half)
+                to, there = beyond(column, place, grid.splits)
+                peer = {"dp": grid.at(to * grid.share + rest, near, core)}
+                send_items(step, items_out.at[place, half], place, peer, there)
+                for k in range(1, grid.halves):
+                    send_items(step, items_out.at[place, half], place, {"tp": (half + k) % grid.halves})
+        if 1 <= step <= WEIGHT_PARTS:
+            spread.third(step - 1)
+    if WEIGHT_PARTS >= parts:
+        spread.third(WEIGHT_PARTS - 1)
+    for part in range(parts):
         for k in range(1, grid.halves):
-            send_items(items_out.at[place, half], place, slot, {"tp": (half + k) % grid.halves})
-            slot += 1
-    for part in range(PARTS):
-        spread.third(part)
-    for k in range(1, grid.halves):
-        for j in range(grid.splits):
-            arrived((column + j) % grid.splits, (half + k) % grid.halves)
+            for j in range(grid.splits):
+                arrived(part, (column + j) % grid.splits, (half + k) % grid.halves)
     for copy in sent:
         copy.wait_send()
+    for when, copy in maybe:
+        pl.when(when)(copy.wait_send)
     own.wait()
     spread.last()
 
 
-def spread_sems(grid):
-    sends = grid.far - 1 + grid.far * (grid.near - 1) + grid.far * grid.near
+def spread_sems(grid, parts):
+    sends = grid.far + 1 + grid.far * (grid.near - 1) + grid.far * grid.near
     return [
-        pltpu.SemaphoreType.DMA((PARTS, sends)),
-        pltpu.SemaphoreType.DMA((PARTS, grid.blocks)),
+        pltpu.SemaphoreType.DMA((parts, sends)),
+        pltpu.SemaphoreType.DMA((parts, grid.blocks)),
         pltpu.SemaphoreType.DMA,
     ]
 
@@ -281,7 +324,7 @@
     base = lax.dynamic_slice_in_dim(partial_value, half * rows_half, rows_half, 0) + lax.dynamic_slice_in_dim(
         item_residual, half * rows_half, rows_half, 0
     ).astype(jnp.float32)
-    sends = splits - 1 + splits * (halves - 1)
+    sends = splits + 1 + splits * (halves - 1)
     normed, weight = pl.pallas_call(
         functools.partial(items_kernel, grid),
         out_shape=(
@@ -295,11 +338,11 @@
             pltpu.VMEM((rows_half, width), jnp.bfloat16),
             pltpu.SemaphoreType.DMA((halves - 1,)),
             pltpu.SemaphoreType.DMA((halves - 1,)),
-            pltpu.SemaphoreType.DMA((sends,)),
-            pltpu.SemaphoreType.DMA((splits, halves)),
+            pltpu.SemaphoreType.DMA((rows_half // ITEM_ROWS, sends)),
+            pltpu.SemaphoreType.DMA((rows_half // ITEM_ROWS, splits, halves)),
             pltpu.SemaphoreType.DMA,
         ]
-        + spread_sems(grid),
+        + spread_sems(grid, WEIGHT_PARTS),
         compiler_params=pltpu.CompilerParams(
             collective_id=0, has_side_effects=True, vmem_limit_bytes=24 << 20
         ),
@@ -314,7 +357,7 @@
         out_shape=jax.ShapeDtypeStruct((devices,) + projected.shape, jnp.bfloat16),
         in_specs=[any_space],
         out_specs=any_space,
-        scratch_shapes=spread_sems(grid),
+        scratch_shapes=spread_sems(grid, TABLE_PARTS),
         compiler_params=pltpu.CompilerParams(collective_id=1, has_side_effects=True),
         name="gather_table",
     )(projected)

time: 248 us -> 219 us (0.88)
  Pallas kernels: 198 us -> 169 us
    pallas_call x1, Pallas kernels: 102 us -> 82.5 us  [per_device(): pl.pallas_call(functools.partial(share_kernel, grid), out_shape=jax.Shape...]
    pallas_call x1, Pallas kernels: 95.7 us -> 86.3 us  [per_device(): pl.pallas_call(functools.partial(items_kernel, grid), out_shape=(jax.Shap...]
where the time goes in v3:
time: 219 us; the launch traced here: 218 us
  Pallas kernels  169 us (77%)
  matrix products  32.3 us (15%)
  local copies, waits for them, and re-layouts  15.4 us (7%)
    pallas_call x1, Pallas kernels, per_device(): pl.pallas_call(functools.partial(items_kernel, grid), out_shape=(jax.Shap...  86.3 us
    pallas_call x1, Pallas kernels, per_device(): pl.pallas_call(functools.partial(share_kernel, grid), out_shape=jax.Shape...  82.5 us
    dot_general x1, matrix products, per_device(): jnp.einsum('rn,snc->rsc', chosen, table, preferred_element_type=jnp.float32)  18.8 us
    reshape x1, local copies, waits for them, and re-layouts, per_device(): return out.reshape(home.shape[0], user_heads, triple)  9.06 us
    dot_general x1, matrix products, per_device(): jnp.dot(attended, item_out_weight, preferred_element_type=jnp.float32)  4.74 us

profile of v3, /device:TPU:1, one launch (start us, length us, event | category | flops | bytes accessed | tf_op | source)
XLA Modules:
  0.0 218.4 jit_solution(16091546662628520468)
XLA Ops:
  0.0 0.0 copy-start
  0.0 0.0 copy-start.2
  0.8 0.7 fusion.24
  1.5 1.1 reshape.49
  2.7 3.2 %fusion.9 = f32[128,8,1,4]{3,2,1,0:T(1,128)} fusion(bf16[128,8,128,1]{2,3,1,0:T(2,128)(2,1)S(1)} %reshape.49, bf16[128,4,1024]{2,1,0:T(4,128)(2,1)} %param.11), kind=kOutput, calls=%fused_computation.9 | convolution fusion | flops 1048576 | bytes 1327104 | tf_op jit(solution)/shard_map/ihd,ithd->iht/dot_general | solution.py:27
  5.9 1.2 copy.23
  7.2 0.4 copy.24
  7.6 0.0 copy-done
  7.6 1.2 fusion.7
  8.9 0.0 copy-done.2
  8.9 1.9 copy.17
  10.8 1.7 copy.18
  12.5 0.0 copy-start.3
  12.5 0.0 copy-start.1
  12.5 4.7 %fusion.30 = (bf16[128,4096]{1,0:T(8,128)(2,1)S(1)}, f32[128,4096]{1,0:T(8,128)S(1)}) fusion(bf16[1024,4096]{1,0:T(8,128)(2,1)} %param.13, bf16[16,8,8,128]{3,2,1,0:T(8,128)(2,1)S(1)} %bitcast.58), kind=kOutput, calls=%fused_computation.46 | convolution fusion | flops 1074266112 | bytes 11796480 | tf_op jit(solution)/shard_map/dot_general | solution.py:322
  17.3 0.0 copy-done.3
  17.3 0.1 convert_add_fusion.base_ref
  17.4 0.0 copy-done.1
  17.4 86.3 %gather_items.1 = (bf16[4,2,64,4096]{3,2,1,0:T(8,128)(2,1)S(1)}, bf16[16,256,768]{2,1,0:T(8,128)(2,1)S(1)}) custom-call(bf16[2,64,4096]{2,1,0:T(8,128)(2,1)S(1)} %bitcast.51, f32[64,4096]{1,0:T(8,128)S(1)} %convert_add_fusion.base_ref, f32[1,4096]{1,0:T(1,128)S(1)} %bitcast.52, bf16[4,256,768]{2,1,0:T(8,128)(2,1)S(1)} %bitcast.50), custom_call_target="tpu_custom_call" | custom-call | tf_op jit(solution)/shard_map/gather_items/pallas_call | solution.py:328
  103.7 4.3 %convolution_convert_fusion.block_ref = bf16[512,768]{1,0:T(8,128)(2,1)} fusion(bf16[512,4096]{1,0:T(8,128)(2,1)S(1)} %bitcast.54, bf16[4096,768]{1,0:T(8,128)(2,1)S(1)} %bitcast.53), kind=kOutput, calls=%fused_computation.5 | convolution fusion | flops 3221618688 | bytes 11272192 | tf_op jit(solution)/shard_map/dot_general | solution.py:354
  108.0 82.5 %gather_table.1 = bf16[16,512,768]{2,1,0:T(8,128)(2,1)} custom-call(bf16[512,768]{1,0:T(8,128)(2,1)} %convolution_convert_fusion.block_ref), custom_call_target="tpu_custom_call" | custom-call | tf_op jit(solution)/shard_map/gather_table/pallas_call | solution.py:355
  190.5 18.8 %fusion.4 = bf16[1024,4,768]{0,2,1:T(8,128)(2,1)} fusion(bf16[4,2048,768]{2,1,0:T(8,128)(2,1)} %bitcast.55, s32[1024]{0:T(1024)S(1)} %fusion.24), kind=kOutput, calls=%fused_computation.4 | convolution fusion | flops 12890144768 | bytes 18878464 | tf_op jit(solution)/shard_map/rn,snc->rsc/dot_general | solution.py:373
  209.4 9.1 %copy.20 = bf16[1024,8,384]{2,1,0:T(8,128)(2,1)} copy(bf16[1024,8,384]{0,2,1:T(8,128)(2,1)} %bitcast.56) | data formatting | bytes 12582912 | tf_op jit(solution)/shard_map/reshape | solution.py:374
  (4 shorter events, 0.1 us)
Async XLA Ops:
  0.0 7.6 %copy-start = (bf16[128,4,1024]{2,1,0:T(4,128)(2,1)S(1)}, bf16[128,4,1024]{2,1,0:T(4,128)(2,1)}, u32[]{:S(2)}) copy-start(bf16[128,4,1024]{2,1,0:T(4,128)(2,1)} %param.12) | copy-start | bytes 3145732
  0.0 8.9 %copy-start.2 = (bf16[256,8,384]{2,1,0:T(8,128)(2,1)S(1)}, bf16[256,8,384]{2,1,0:T(8,128)(2,1)}, u32[]{:S(2)}) copy-start(bf16[256,8,384]{2,1,0:T(8,128)(2,1)} %param.19) | copy-start | bytes 4718596
  12.5 4.8 %copy-start.3 = (bf16[128,4096]{1,0:T(8,128)(2,1)S(1)}, bf16[128,4096]{1,0:T(8,128)(2,1)}, u32[]{:S(2)}) copy-start(bf16[128,4096]{1,0:T(8,128)(2,1)} %param.14) | copy-start | bytes 3145732
  12.5 4.9 %copy-start.1 = (f32[4096]{0:T(1024)S(1)}, f32[4096]{0:T(1024)}, u32[]{:S(2)}) copy-start(f32[4096]{0:T(1024)} %param.18) | copy-start | bytes 49156
